TPU v7x, 128 devices: a whole 4x4x4 slice. The times are simulated.
128 devices in a mesh: grp: 16 (over z, y), dp: 8 (over x, core).
Axes of the slice: x: 4, y: 4, z: 4, core: 2. Of those that a mesh axis runs over, the one named last changes fastest.
Arguments:
- query_rows: bfloat16 [8, 4, 1024, 4096], P('dp', None, 'grp'), may hold values from -80 to 80
- key_rows: bfloat16 [8, 4, 1024, 1024], P('dp', None, 'grp'), may hold values from -4 to 4
- value_rows: bfloat16 [8, 4, 1024, 1024], P('dp', None, 'grp'), may hold values from -6 to 6
- segment_ids: int32 [4, 8192], replicated, may hold values from 0 to 2, never falling along the last dimension, each value on 1 to 5461 neighbouring positions
Outputs:
- attended: bfloat16 [8, 4, 1024, 4096], P('dp', None, 'grp')
All inputs are finite; a program needn't handle non-finite values.
Results may differ from a plain program's by a relative error of at most 0.0039.
Values may be sent and summed in bfloat16 or wider, within the bound.
A program may use at most 64 MiB of HBM per device.

v0:
```python
import jax
import jax.numpy as jnp
from jax import lax
from jax.sharding import PartitionSpec as P

HEAD_DIM = 128


def widen_heads(values, repeat):
    count = values.shape[-1] // HEAD_DIM
    split = values.reshape(values.shape[:-1] + (count, HEAD_DIM))
    grown = jnp.repeat(split, repeat, axis=-2)
    return grown.reshape(values.shape[:-1] + (count * repeat * HEAD_DIM,))


def halves_first(values):
    groups_n, rows_n, feature_n = (values.shape[1], values.shape[2], values.shape[3])
    split = values.reshape(1, groups_n, rows_n, 2, feature_n // 2)
    moved = jnp.transpose(split, (0, 1, 3, 2, 4))
    return moved.reshape(1, 2 * groups_n, rows_n, feature_n // 2)


def attend(queries, keyset, valueset, labels):
    seq_len = queries.shape[0]
    heads_n = queries.shape[1]
    block = min(512, seq_len)
    factor = 1.0 / HEAD_DIM**0.5

    def one_block(index):
        start = index * block
        query_block = lax.dynamic_slice_in_dim(queries, start, block, 0)
        label_block = lax.dynamic_slice_in_dim(labels, start, block, 0)
        rows_pos = start + jnp.arange(block, dtype=jnp.int32)

        def key_scores(other):
            key_start = other * block
            key_block = lax.dynamic_slice_in_dim(keyset, key_start, block, 0)
            key_labels = lax.dynamic_slice_in_dim(labels, key_start, block, 0)
            key_pos = key_start + jnp.arange(block, dtype=jnp.int32)
            allowed = (label_block[:, None] == key_labels[None, :]) & (
                rows_pos[:, None] >= key_pos[None, :]
            )
            scores = (
                jnp.einsum(
                    "qhd,khd->hqk", query_block, key_block, preferred_element_type=jnp.float32
                )
                * factor
            )
            return (jnp.where(allowed[None], scores, -1e30), allowed)

        def max_step(other, current):
            scores, allowed = key_scores(other)
            return jnp.maximum(current, jnp.max(scores, axis=2, keepdims=True))

        largest = lax.fori_loop(
            0, index + 1, max_step, jnp.full((heads_n, block, 1), -1e30, jnp.float32)
        )

        def sum_step(other, carry):
            total, summed = carry
            scores, allowed = key_scores(other)
            weights = jnp.where(allowed[None], jnp.exp(scores - largest), 0.0)
            value_block = lax.dynamic_slice_in_dim(valueset, other * block, block, 0)
            rounded = weights.astype(jnp.bfloat16)
            summed = summed + jnp.einsum(
                "hqk,khd->qhd", rounded, value_block, preferred_element_type=jnp.float32
            )
            return (total + jnp.sum(weights, axis=2, keepdims=True), summed)

        start_carry = (
            jnp.zeros((heads_n, block, 1), jnp.float32),
            jnp.zeros((block, heads_n, HEAD_DIM), jnp.float32),
        )
        total, summed = lax.fori_loop(0, index + 1, sum_step, start_carry)
        return (summed / jnp.transpose(total, (1, 0, 2))).astype(jnp.bfloat16)

    blocks = lax.map(one_block, jnp.arange(seq_len // block, dtype=jnp.int32))
    return blocks.reshape(seq_len, heads_n * HEAD_DIM)


def per_device(query_rows, key_rows, value_rows, segment_ids):
    width_n = lax.axis_size("grp")
    loaders = lax.axis_size("dp")
    groups_n = query_rows.shape[1]
    rows_n = query_rows.shape[2]
    members = 2 * width_n
    kv_total = key_rows.shape[-1] // HEAD_DIM
    repeat = max(1, members // kv_total)
    key_wide = widen_heads(key_rows, repeat)
    value_wide = widen_heads(value_rows, repeat)
    sectioned = (
        lax.all_to_all(
            lax.all_to_all(
                halves_first(query_rows), "grp", split_axis=3, concat_axis=2, tiled=True
            ),
            "dp",
            split_axis=1,
            concat_axis=0,
            tiled=True,
        ),
        lax.all_to_all(
            lax.all_to_all(halves_first(key_wide), "grp", split_axis=3, concat_axis=2, tiled=True),
            "dp",
            split_axis=1,
            concat_axis=0,
            tiled=True,
        ),
        lax.all_to_all(
            lax.all_to_all(
                halves_first(value_wide), "grp", split_axis=3, concat_axis=2, tiled=True
            ),
            "dp",
            split_axis=1,
            concat_axis=0,
            tiled=True,
        ),
    )
    query_here = sectioned[0].reshape(-1, sectioned[0].shape[-1])
    key_here = sectioned[1].reshape(-1, sectioned[1].shape[-1])
    value_here = sectioned[2].reshape(-1, sectioned[2].shape[-1])
    seq_len = query_here.shape[0]
    local_heads = query_here.shape[-1] // HEAD_DIM
    local_kv = key_here.shape[-1] // HEAD_DIM
    queries = query_here.reshape(seq_len, local_heads, HEAD_DIM)
    keyset = jnp.repeat(
        key_here.reshape(seq_len, local_kv, HEAD_DIM), local_heads // local_kv, axis=1
    )
    valueset = jnp.repeat(
        value_here.reshape(seq_len, local_kv, HEAD_DIM), local_heads // local_kv, axis=1
    )
    group_here = lax.axis_index("dp") // 2
    labels = lax.dynamic_index_in_dim(segment_ids, group_here, 0, keepdims=False)
    output = attend(queries, keyset, valueset, labels)
    piece = local_heads * HEAD_DIM
    shaped = output.reshape(loaders, 1, width_n * rows_n, piece)
    back = lax.all_to_all(
        lax.all_to_all(shaped, "grp", split_axis=2, concat_axis=3, tiled=True),
        "dp",
        split_axis=0,
        concat_axis=1,
        tiled=True,
    )
    ordered = jnp.transpose(back.reshape(1, groups_n, 2, rows_n, width_n * piece), (0, 1, 3, 2, 4))
    return ordered.reshape(1, groups_n, rows_n, 2 * width_n * piece)


def solution(mesh):
    return jax.shard_map(
        per_device,
        mesh=mesh,
        in_specs=(
            P("dp", None, "grp", None),
            P("dp", None, "grp", None),
            P("dp", None, "grp", None),
            P(),
        ),
        out_specs=P("dp", None, "grp", None),
        check_vma=False,
    )
```

profile of v0, /device:TPU:1, one launch (start us, length us, event | category | flops | bytes accessed | tf_op | source)
XLA Modules:
  0.0 783.2 jit_solution(15200198801345029798)
XLA Ops:
  2.0 4.3 copy.42
  6.3 7.5 reshape.115
  13.8 8.7 %all-to-all-start = ((bf16[16,2,32768]{2,1,0:T(2,128)(2,1)}), bf16[16,2,32768]{2,1,0:T(2,128)(2,1)S(1)}, u32[]{:S(2)}, u32[]{:S(2)}) async-start(bf16[16,2,32768]{2,1,0:T(2,128)(2,1)} %reshape.115), calls=%async_computation | async-start | bytes 4194304 | tf_op jit(solution)/shard_map/all_to_all | solution.py:93
  22.6 2.1 broadcast_in_dim.45
  24.7 4.0 broadcast_in_dim.46
  28.7 3.8 copy.46
  32.5 5.7 copy.47
  38.2 7.5 reshape.117
  45.7 7.3 all-to-all-done
  53.0 4.4 all-to-all-start.2
  59.6 4.0 broadcast_in_dim.48
  63.6 3.8 copy.51
  67.4 5.7 copy.52
  73.1 7.5 reshape.119
  80.6 3.6 all-to-all-done.2
  84.2 7.0 all-to-all-start.4
  91.1 5.0 reshape.116
  96.2 4.9 copy.61
  103.0 14.7 %all-to-all-done.4 = bf16[16,2,32768]{2,1,0:T(2,128)(2,1)} async-done(((bf16[16,2,32768]{2,1,0:T(2,128)(2,1)}), bf16[16,2,32768]{2,1,0:T(2,128)(2,1)}, u32[]{:S(2)}, u32[]{:S(2)}) %all-to-all-start.4) | async-done | bytes 2097184 | tf_op jit(solution)/shard_map/all_to_all | solution.py:109
  117.7 9.3 %all-to-all-start.1 = ((bf16[1,8,1024,128]{3,2,0,1:T(8,128)(2,1)}), bf16[1,8,1024,128]{3,2,0,1:T(8,128)(2,1)}, u32[]{:S(2)}, u32[]{:S(2)}) async-start(bf16[1,8,1024,128]{3,2,0,1:T(8,128)(2,1)} %bitcast.149), calls=%async_computation.1 | async-start | bytes 4194304 | tf_op jit(solution)/shard_map/all_to_all | solution.py:92
  127.0 7.4 reshape.118
  134.3 4.9 copy.62
  141.2 12.2 %all-to-all-done.1 = bf16[1,8,1024,128]{3,2,0,1:T(8,128)(2,1)} async-done(((bf16[1,8,1024,128]{3,2,0,1:T(8,128)(2,1)}), bf16[1,8,1024,128]{3,2,0,1:T(8,128)(2,1)}, u32[]{:S(2)}, u32[]{:S(2)}) %all-to-all-start.1) | async-done | bytes 2097184 | tf_op jit(solution)/shard_map/all_to_all | solution.py:92
  153.4 5.1 all-to-all-start.3
  158.5 7.4 reshape.120
  165.9 4.9 copy.63
  172.8 12.2 %all-to-all-done.3 = bf16[1,8,1024,128]{3,2,0,1:T(8,128)(2,1)} async-done(((bf16[1,8,1024,128]{3,2,0,1:T(8,128)(2,1)}), bf16[1,8,1024,128]{3,2,0,1:T(8,128)(2,1)}, u32[]{:S(2)}, u32[]{:S(2)}) %all-to-all-start.3) | async-done | bytes 2097184 | tf_op jit(solution)/shard_map/all_to_all | solution.py:101
  185.0 4.4 all-to-all-start.5
  189.4 26.3 %all-to-all-done.5 = bf16[1,8,1024,128]{3,2,0,1:T(8,128)(2,1)S(1)} async-done(((bf16[1,8,1024,128]{3,2,0,1:T(8,128)(2,1)}), bf16[1,8,1024,128]{3,2,0,1:T(8,128)(2,1)S(1)}, u32[]{:S(2)}, u32[]{:S(2)}) %all-to-all-start.5) | async-done | bytes 2097184 | tf_op jit(solution)/shard_map/all_to_all | solution.py:108
  215.7 497.5 %while.36 = (s32[]{:T(128)}, bf16[16,512,1,128]{3,1,0,2:T(8,128)(2,1)}, s32[16]{0:T(128)S(1)}, s32[8192]{0:T(1024)S(1)}, bf16[8192,1,128]{2,0,1:T(8,128)(2,1)}, ...) while((s32[]{:T(128)}, ...), condition=%wide.region_7.8_spmd, body=%wide.region_0.7_spmd.sunk | while | flops 205457424 | bytes 3732873 | solution.py:77
  225.3 2.8 while.37
  228.2 3.6 while.38
  235.3 4.2 while.37
  239.6 5.5 while.38
  248.7 5.7 while.37
  254.4 7.3 while.38
  265.2 7.1 while.37
  272.3 9.1 %while.38 = (s32[]{:T(128)}, f32[1,512,1]{1,2,0:T(1,128)S(1)}, f32[512,1,128]{0,2,1:T(8,128)S(1)}, s32[]{:T(128)}, s32[512]{0:T(512)S(1)}, /*index=5*/s32[8192]{...) while((s32[]{:T(128)}, f32[1,512,1]{1,2,0:T(1,128)S(1)}, ...), condition=%wide.region_6.6_spmd.clone, body=%wide.region_4.5_spmd.clone.sunk | while | flops 136643584 | bytes 1992911 | solution.py:74
  285.0 8.5 %while.37 = (s32[]{:T(128)}, f32[1,512,1]{1,2,0:T(1,128)S(1)}, s32[]{:T(128)}, s32[512]{0:T(512)S(1)}, s32[8192]{0:T(1024)S(1)}, /*index=5*/bf16[8192,1,128]{2,0...) while((s32[]{:T(128)}, f32[1,512,1]{1,2,0:T(1,128)S(1)}, ...), condition=%wide.region_3.3_spmd.clone, body=%wide.region_1.2_spmd.clone.sunk | while | flops 68682760 | bytes 286899 | solution.py:55
  293.5 10.9 %while.38 = (s32[]{:T(128)}, f32[1,512,1]{1,2,0:T(1,128)S(1)}, f32[512,1,128]{0,2,1:T(8,128)S(1)}, s32[]{:T(128)}, s32[512]{0:T(512)S(1)}, /*index=5*/s32[8192]{...) while((s32[]{:T(128)}, f32[1,512,1]{1,2,0:T(1,128)S(1)}, ...), condition=%wide.region_6.6_spmd.clone, body=%wide.region_4.5_spmd.clone.sunk | while | flops 136643584 | bytes 1992911 | solution.py:74
  308.0 9.9 %while.37 = (s32[]{:T(128)}, f32[1,512,1]{1,2,0:T(1,128)S(1)}, s32[]{:T(128)}, s32[512]{0:T(512)S(1)}, s32[8192]{0:T(1024)S(1)}, /*index=5*/bf16[8192,1,128]{2,0...) while((s32[]{:T(128)}, f32[1,512,1]{1,2,0:T(1,128)S(1)}, ...), condition=%wide.region_3.3_spmd.clone, body=%wide.region_1.2_spmd.clone.sunk | while | flops 68682760 | bytes 286899 | solution.py:55
  318.0 12.7 %while.38 = (s32[]{:T(128)}, f32[1,512,1]{1,2,0:T(1,128)S(1)}, f32[512,1,128]{0,2,1:T(8,128)S(1)}, s32[]{:T(128)}, s32[512]{0:T(512)S(1)}, /*index=5*/s32[8192]{...) while((s32[]{:T(128)}, f32[1,512,1]{1,2,0:T(1,128)S(1)}, ...), condition=%wide.region_6.6_spmd.clone, body=%wide.region_4.5_spmd.clone.sunk | while | flops 136643584 | bytes 1992911 | solution.py:74
  334.3 11.3 %while.37 = (s32[]{:T(128)}, f32[1,512,1]{1,2,0:T(1,128)S(1)}, s32[]{:T(128)}, s32[512]{0:T(512)S(1)}, s32[8192]{0:T(1024)S(1)}, /*index=5*/bf16[8192,1,128]{2,0...) while((s32[]{:T(128)}, f32[1,512,1]{1,2,0:T(1,128)S(1)}, ...), condition=%wide.region_3.3_spmd.clone, body=%wide.region_1.2_spmd.clone.sunk | while | flops 68682760 | bytes 286899 | solution.py:55
  345.6 14.5 %while.38 = (s32[]{:T(128)}, f32[1,512,1]{1,2,0:T(1,128)S(1)}, f32[512,1,128]{0,2,1:T(8,128)S(1)}, s32[]{:T(128)}, s32[512]{0:T(512)S(1)}, /*index=5*/s32[8192]{...) while((s32[]{:T(128)}, f32[1,512,1]{1,2,0:T(1,128)S(1)}, ...), condition=%wide.region_6.6_spmd.clone, body=%wide.region_4.5_spmd.clone.sunk | while | flops 136643584 | bytes 1992911 | solution.py:74
  363.7 12.7 %while.37 = (s32[]{:T(128)}, f32[1,512,1]{1,2,0:T(1,128)S(1)}, s32[]{:T(128)}, s32[512]{0:T(512)S(1)}, s32[8192]{0:T(1024)S(1)}, /*index=5*/bf16[8192,1,128]{2,0...) while((s32[]{:T(128)}, f32[1,512,1]{1,2,0:T(1,128)S(1)}, ...), condition=%wide.region_3.3_spmd.clone, body=%wide.region_1.2_spmd.clone.sunk | while | flops 68682760 | bytes 286899 | solution.py:55
  376.5 16.4 %while.38 = (s32[]{:T(128)}, f32[1,512,1]{1,2,0:T(1,128)S(1)}, f32[512,1,128]{0,2,1:T(8,128)S(1)}, s32[]{:T(128)}, s32[512]{0:T(512)S(1)}, /*index=5*/s32[8192]{...) while((s32[]{:T(128)}, f32[1,512,1]{1,2,0:T(1,128)S(1)}, ...), condition=%wide.region_6.6_spmd.clone, body=%wide.region_4.5_spmd.clone.sunk | while | flops 136643584 | bytes 1992911 | solution.py:74
  396.4 14.2 %while.37 = (s32[]{:T(128)}, f32[1,512,1]{1,2,0:T(1,128)S(1)}, s32[]{:T(128)}, s32[512]{0:T(512)S(1)}, s32[8192]{0:T(1024)S(1)}, /*index=5*/bf16[8192,1,128]{2,0...) while((s32[]{:T(128)}, f32[1,512,1]{1,2,0:T(1,128)S(1)}, ...), condition=%wide.region_3.3_spmd.clone, body=%wide.region_1.2_spmd.clone.sunk | while | flops 68682760 | bytes 286899 | solution.py:55
  410.6 18.2 %while.38 = (s32[]{:T(128)}, f32[1,512,1]{1,2,0:T(1,128)S(1)}, f32[512,1,128]{0,2,1:T(8,128)S(1)}, s32[]{:T(128)}, s32[512]{0:T(512)S(1)}, /*index=5*/s32[8192]{...) while((s32[]{:T(128)}, f32[1,512,1]{1,2,0:T(1,128)S(1)}, ...), condition=%wide.region_6.6_spmd.clone, body=%wide.region_4.5_spmd.clone.sunk | while | flops 136643584 | bytes 1992911 | solution.py:74
  432.4 15.6 %while.37 = (s32[]{:T(128)}, f32[1,512,1]{1,2,0:T(1,128)S(1)}, s32[]{:T(128)}, s32[512]{0:T(512)S(1)}, s32[8192]{0:T(1024)S(1)}, /*index=5*/bf16[8192,1,128]{2,0...) while((s32[]{:T(128)}, f32[1,512,1]{1,2,0:T(1,128)S(1)}, ...), condition=%wide.region_3.3_spmd.clone, body=%wide.region_1.2_spmd.clone.sunk | while | flops 68682760 | bytes 286899 | solution.py:55
  448.0 20.0 %while.38 = (s32[]{:T(128)}, f32[1,512,1]{1,2,0:T(1,128)S(1)}, f32[512,1,128]{0,2,1:T(8,128)S(1)}, s32[]{:T(128)}, s32[512]{0:T(512)S(1)}, /*index=5*/s32[8192]{...) while((s32[]{:T(128)}, f32[1,512,1]{1,2,0:T(1,128)S(1)}, ...), condition=%wide.region_6.6_spmd.clone, body=%wide.region_4.5_spmd.clone.sunk | while | flops 136643584 | bytes 1992911 | solution.py:74
  471.5 17.0 %while.37 = (s32[]{:T(128)}, f32[1,512,1]{1,2,0:T(1,128)S(1)}, s32[]{:T(128)}, s32[512]{0:T(512)S(1)}, s32[8192]{0:T(1024)S(1)}, /*index=5*/bf16[8192,1,128]{2,0...) while((s32[]{:T(128)}, f32[1,512,1]{1,2,0:T(1,128)S(1)}, ...), condition=%wide.region_3.3_spmd.clone, body=%wide.region_1.2_spmd.clone.sunk | while | flops 68682760 | bytes 286899 | solution.py:55
  488.6 21.8 %while.38 = (s32[]{:T(128)}, f32[1,512,1]{1,2,0:T(1,128)S(1)}, f32[512,1,128]{0,2,1:T(8,128)S(1)}, s32[]{:T(128)}, s32[512]{0:T(512)S(1)}, /*index=5*/s32[8192]{...) while((s32[]{:T(128)}, f32[1,512,1]{1,2,0:T(1,128)S(1)}, ...), condition=%wide.region_6.6_spmd.clone, body=%wide.region_4.5_spmd.clone.sunk | while | flops 136643584 | bytes 1992911 | solution.py:74
  514.0 18.4 %while.37 = (s32[]{:T(128)}, f32[1,512,1]{1,2,0:T(1,128)S(1)}, s32[]{:T(128)}, s32[512]{0:T(512)S(1)}, s32[8192]{0:T(1024)S(1)}, /*index=5*/bf16[8192,1,128]{2,0...) while((s32[]{:T(128)}, f32[1,512,1]{1,2,0:T(1,128)S(1)}, ...), condition=%wide.region_3.3_spmd.clone, body=%wide.region_1.2_spmd.clone.sunk | while | flops 68682760 | bytes 286899 | solution.py:55
  532.4 23.6 %while.38 = (s32[]{:T(128)}, f32[1,512,1]{1,2,0:T(1,128)S(1)}, f32[512,1,128]{0,2,1:T(8,128)S(1)}, s32[]{:T(128)}, s32[512]{0:T(512)S(1)}, /*index=5*/s32[8192]{...) while((s32[]{:T(128)}, f32[1,512,1]{1,2,0:T(1,128)S(1)}, ...), condition=%wide.region_6.6_spmd.clone, body=%wide.region_4.5_spmd.clone.sunk | while | flops 136643584 | bytes 1992911 | solution.py:74
  559.6 19.8 %while.37 = (s32[]{:T(128)}, f32[1,512,1]{1,2,0:T(1,128)S(1)}, s32[]{:T(128)}, s32[512]{0:T(512)S(1)}, s32[8192]{0:T(1024)S(1)}, /*index=5*/bf16[8192,1,128]{2,0...) while((s32[]{:T(128)}, f32[1,512,1]{1,2,0:T(1,128)S(1)}, ...), condition=%wide.region_3.3_spmd.clone, body=%wide.region_1.2_spmd.clone.sunk | while | flops 68682760 | bytes 286899 | solution.py:55
  579.4 25.4 %while.38 = (s32[]{:T(128)}, f32[1,512,1]{1,2,0:T(1,128)S(1)}, f32[512,1,128]{0,2,1:T(8,128)S(1)}, s32[]{:T(128)}, s32[512]{0:T(512)S(1)}, /*index=5*/s32[8192]{...) while((s32[]{:T(128)}, f32[1,512,1]{1,2,0:T(1,128)S(1)}, ...), condition=%wide.region_6.6_spmd.clone, body=%wide.region_4.5_spmd.clone.sunk | while | flops 136643584 | bytes 1992911 | solution.py:74
  608.5 21.2 %while.37 = (s32[]{:T(128)}, f32[1,512,1]{1,2,0:T(1,128)S(1)}, s32[]{:T(128)}, s32[512]{0:T(512)S(1)}, s32[8192]{0:T(1024)S(1)}, /*index=5*/bf16[8192,1,128]{2,0...) while((s32[]{:T(128)}, f32[1,512,1]{1,2,0:T(1,128)S(1)}, ...), condition=%wide.region_3.3_spmd.clone, body=%wide.region_1.2_spmd.clone.sunk | while | flops 68682760 | bytes 286899 | solution.py:55
  629.7 27.3 %while.38 = (s32[]{:T(128)}, f32[1,512,1]{1,2,0:T(1,128)S(1)}, f32[512,1,128]{0,2,1:T(8,128)S(1)}, s32[]{:T(128)}, s32[512]{0:T(512)S(1)}, /*index=5*/s32[8192]{...) while((s32[]{:T(128)}, f32[1,512,1]{1,2,0:T(1,128)S(1)}, ...), condition=%wide.region_6.6_spmd.clone, body=%wide.region_4.5_spmd.clone.sunk | while | flops 136643584 | bytes 1992911 | solution.py:74
  660.6 22.6 %while.37 = (s32[]{:T(128)}, f32[1,512,1]{1,2,0:T(1,128)S(1)}, s32[]{:T(128)}, s32[512]{0:T(512)S(1)}, s32[8192]{0:T(1024)S(1)}, /*index=5*/bf16[8192,1,128]{2,0...) while((s32[]{:T(128)}, f32[1,512,1]{1,2,0:T(1,128)S(1)}, ...), condition=%wide.region_3.3_spmd.clone, body=%wide.region_1.2_spmd.clone.sunk | while | flops 68682760 | bytes 286899 | solution.py:55
  683.2 29.1 %while.38 = (s32[]{:T(128)}, f32[1,512,1]{1,2,0:T(1,128)S(1)}, f32[512,1,128]{0,2,1:T(8,128)S(1)}, s32[]{:T(128)}, s32[512]{0:T(512)S(1)}, /*index=5*/s32[8192]{...) while((s32[]{:T(128)}, f32[1,512,1]{1,2,0:T(1,128)S(1)}, ...), condition=%wide.region_6.6_spmd.clone, body=%wide.region_4.5_spmd.clone.sunk | while | flops 136643584 | bytes 1992911 | solution.py:74
  713.2 2.9 copy.57
  716.1 30.0 %all_to_all.108 = bf16[8,1,1024,128]{3,0,1,2:T(8,128)(2,1)S(1)} all-to-all(bf16[8,1,1024,128]{3,0,1,2:T(8,128)(2,1)S(1)} %copy.57), channel_id=1, replica_groups=mesh['grp'=16,'dp'=8] {'grp'}, dimensions={2} | all-to-all | bytes 4194304 | tf_op jit(solution)/shard_map/all_to_all | solution.py:137
  747.5 2.3 all_to_all.98
  749.8 31.9 %all_to_all.109 = bf16[8,1,64,2048]{3,2,1,0:T(8,128)(2,1)S(1)} all-to-all(bf16[8,1,64,2048]{3,2,1,0:T(8,128)(2,1)} %bitcast.155), channel_id=1, replica_groups=mesh['grp'=16,'dp'=8] {'dp'}, dimensions={0} | all-to-all | bytes 4194304 | tf_op jit(solution)/shard_map/all_to_all | solution.py:136
  (1391 shorter events, 484.4 us)
Async XLA Ops:
  0.0 189.3 %copy-start = (s32[4,8192]{1,0:T(4,128)S(1)}, s32[4,8192]{1,0:T(4,128)}, u32[]{:S(2)}) copy-start(s32[4,8192]{1,0:T(4,128)} %param.13) | copy-start | bytes 393220
  13.8 8.7 %copy-start.2 = (bf16[1,4,64,1024]{3,2,1,0:T(8,128)(2,1)S(1)}, bf16[1,4,64,1024]{3,2,1,0:T(8,128)(2,1)}, u32[]{:S(2)}) copy-start(bf16[1,4,64,1024]{3,2,1,0:T(8,128)(2,1)} %param.11) | copy-start | bytes 1572868
  13.8 39.2 %all-to-all-start = ((bf16[16,2,32768]{2,1,0:T(2,128)(2,1)}), bf16[16,2,32768]{2,1,0:T(2,128)(2,1)S(1)}, u32[]{:S(2)}, u32[]{:S(2)}) async-start(bf16[16,2,32768]{2,1,0:T(2,128)(2,1)} %reshape.115), calls=%async_computation | async-start | bytes 4194304 | tf_op jit(solution)/shard_map/all_to_all | solution.py:93
  45.7 11.7 %copy-start.3 = (bf16[1,4,64,1024]{3,2,1,0:T(8,128)(2,1)S(1)}, bf16[1,4,64,1024]{3,2,1,0:T(8,128)(2,1)}, u32[]{:S(2)}) copy-start(bf16[1,4,64,1024]{3,2,1,0:T(8,128)(2,1)} %param.12) | copy-start | bytes 1572868
  53.0 31.2 %all-to-all-start.2 = ((bf16[16,2,32768]{2,1,0:T(2,128)(2,1)}), bf16[16,2,32768]{2,1,0:T(2,128)(2,1)}, u32[]{:S(2)}, u32[]{:S(2)}) async-start(bf16[16,2,32768]{2,1,0:T(2,128)(2,1)} %reshape.117), calls=%async_computation.2 | async-start | bytes 4194304 | tf_op jit(solution)/shard_map/all_to_all | solution.py:102
  84.2 33.5 %all-to-all-start.4 = ((bf16[16,2,32768]{2,1,0:T(2,128)(2,1)}), bf16[16,2,32768]{2,1,0:T(2,128)(2,1)}, u32[]{:S(2)}, u32[]{:S(2)}) async-start(bf16[16,2,32768]{2,1,0:T(2,128)(2,1)} %reshape.119), calls=%async_computation.4 | async-start | bytes 4194304 | tf_op jit(solution)/shard_map/all_to_all | solution.py:109
  117.7 35.7 %all-to-all-start.1 = ((bf16[1,8,1024,128]{3,2,0,1:T(8,128)(2,1)}), bf16[1,8,1024,128]{3,2,0,1:T(8,128)(2,1)}, u32[]{:S(2)}, u32[]{:S(2)}) async-start(bf16[1,8,1024,128]{3,2,0,1:T(8,128)(2,1)} %bitcast.149), calls=%async_computation.1 | async-start | bytes 4194304 | tf_op jit(solution)/shard_map/all_to_all | solution.py:92
  153.4 31.6 %all-to-all-start.3 = ((bf16[1,8,1024,128]{3,2,0,1:T(8,128)(2,1)}), bf16[1,8,1024,128]{3,2,0,1:T(8,128)(2,1)}, u32[]{:S(2)}, u32[]{:S(2)}) async-start(bf16[1,8,1024,128]{3,2,0,1:T(8,128)(2,1)} %bitcast.150), calls=%async_computation.3 | async-start | bytes 4194304 | tf_op jit(solution)/shard_map/all_to_all | solution.py:101
  185.0 30.7 %all-to-all-start.5 = ((bf16[1,8,1024,128]{3,2,0,1:T(8,128)(2,1)}), bf16[1,8,1024,128]{3,2,0,1:T(8,128)(2,1)S(1)}, u32[]{:S(2)}, u32[]{:S(2)}) async-start(bf16[1,8,1024,128]{3,2,0,1:T(8,128)(2,1)} %bitcast.148), calls=%async_computation.5 | async-start | bytes 4194304 | tf_op jit(solution)/shard_map/all_to_all | solution.py:108
  781.7 1.5 copy-start.1
where the time goes:
time: 790 us; the launch traced here: 783 us
  matrix products  404 us (51%)
  local copies, waits for them, and re-layouts  168 us (21%)
  waiting for transfers between devices  76.3 us (10%)
  blocking collectives  61.9 us (8%)
  starting transfers between devices  38.9 us (5%)
  loops' own time  29.1 us (4%)
    dot_general x272, matrix products, key_scores(): jnp.einsum('qhd,khd->hqk', query_block, key_block, preferred_element_type...  367 us
    unnamed x16, local copies, waits for them, and re-layouts  42.6 us
    dot_general x136, matrix products, sum_step(): jnp.einsum('hqk,khd->qhd', rounded, value_block, preferred_element_type=j...  37.1 us
    all_to_all x1, blocking collectives, per_device(): lax.all_to_all(lax.all_to_all(shaped, 'grp', split_axis=2, concat_axis=3,...  31.9 us
    all_to_all x1, blocking collectives, per_device(): lax.all_to_all(shaped, 'grp', split_axis=2, concat_axis=3, tiled=True)  30 us
    all_to_all x1, waiting for transfers between devices, per_device(): lax.all_to_all(lax.all_to_all(halves_first(value_wide), 'grp', split_axis...  26.3 us
    dynamic_slice x272, local copies, waits for them, and re-layouts, key_scores(): key_labels = lax.dynamic_slice_in_dim(labels, key_start, block, 0)  21.5 us
    another operation x1, loops' own time, attend(): blocks = lax.map(one_block, jnp.arange(seq_len // block, dtype=jnp.int32))  19.1 us
  transfers between devices with their start and end apart: 6, of which 6 were waited for; matrix products, arithmetic and copies ran while one was open for 11% of the time, Pallas kernels for 0%

commit v1 on v0

v1 whole, which is shorter than its diff:
```python
import functools
import math

import jax
import jax.numpy as jnp
import numpy as np
from jax import lax
from jax.experimental import pallas as pl
from jax.experimental.pallas import tpu as pltpu
from jax.sharding import PartitionSpec as P

MESH = pl.DeviceIdType.MESH
SEQ = 8192
ROWS = 64
SHARE = 4
D = 128
L = SHARE * ROWS
TILES = 32
B = 512
NPAT = B // ROWS
VR = D + 16
BIG = float(2**20)
LONGEST = 5461
FACTOR = float(np.log2(np.e) / math.sqrt(D))


def worst_steps():
    worst = 0
    for y in range(4):
        first = (4 * np.arange(TILES) + y) * ROWS
        k1 = first // B
        cuts = np.arange(1, SEQ // ROWS) * ROWS
        best = 0
        for s1 in range(1, LONGEST + 1, 32):
            for s2 in range(max(s1 + 1, SEQ - LONGEST), min(s1 + LONGEST, SEQ - 1) + 1, 32):
                start = np.where(first >= s2, s2, np.where(first >= s1, s1, 0))
                best = max(best, int((k1 - start // B + 1).sum()))
        worst = max(worst, best)
    return worst


SLOTS = 192


def where_am_i():
    gi, di = lax.axis_index("grp"), lax.axis_index("dp")
    return di // 2, gi % 4, gi // 4, di % 2


def greet(x, y, z, c, ring):
    barrier = pltpu.get_barrier_semaphore()
    n = 0
    for dx in range(4):
        for dc in range(2):
            for dz in range(4):
                if dx or dc or dz:
                    to = (((z + dz) % 4) * 4 + y, ((x + dx) % 4) * 2 + (c + dc) % 2)
                    pl.semaphore_signal(barrier, inc=1, device_id=to, device_id_type=MESH)
                    n += 1
    if ring:
        for dy in (1, 3):
            to = (z * 4 + (y + dy) % 4, x * 2 + c)
            pl.semaphore_signal(barrier, inc=1, device_id=to, device_id_type=MESH)
            n += 1
    pl.semaphore_wait(barrier, n)


def drain(ref, sem):
    pltpu.make_async_copy(ref, ref, sem).wait()


def gather_kernel(q_ref, k_ref, v_ref, qo, ko, vo, sk, sv, sq, rk, rv, rq, fk, fv, fs, hk, hv, hs):
    x, y, z, c = where_am_i()
    me = x * 2 + c
    greet(x, y, z, c, True)

    def spread(src, dst, width, send, recv):
        for dx in range(4):
            for dc in range(2):
                i = dx * 2 + dc
                for dz in range(4):
                    g, c2, z2 = (x + dx) % 4, (c + dc) % 2, (z + dz) % 4
                    cols = pl.ds(pl.multiple_of((z2 * 2 + c2) * width, 128), width)
                    if dx or dc or dz:
                        pltpu.make_async_remote_copy(
                            src_ref=src.at[0, g, :, cols],
                            dst_ref=dst,
                            send_sem=send.at[i],
                            recv_sem=recv.at[i],
                            device_id=(z2 * 4 + y, g * 2 + c2),
                            device_id_type=MESH,
                        ).start()
                    else:
                        pltpu.make_async_copy(src.at[0, g, :, cols], dst, recv.at[i]).start()

    spread(k_ref, ko.at[me, z, y], D, sk, rk)
    spread(v_ref, vo.at[me, z, y], D, sv, rv)
    spread(q_ref, qo.at[me, z], SHARE * D, sq, rq)

    up, down, far = (y + 1) % 4, (y + 3) % 4, (y + 2) % 4

    def loader(i):
        return ((x + 4 - i // 2) % 4) * 2 + (c + i % 2) % 2

    def push(ref, to, send, recv):
        pltpu.make_async_remote_copy(
            src_ref=ref,
            dst_ref=ref,
            send_sem=send,
            recv_sem=recv,
            device_id=(z * 4 + to, me),
            device_id_type=MESH,
        ).start()

    for i in range(8):
        l = loader(i)
        for buf, recv, fwd, o in ((ko, rk, fk, 0), (vo, rv, fv, 2)):
            part = buf.at[l, :, y]
            drain(part, recv.at[i])
            push(part, up, fs.at[o, i], fwd.at[0, i])
            push(part, down, fs.at[o + 1, i], fwd.at[1, i])
    for i in range(8):
        l = loader(i)
        part = ko.at[l, :, down]
        drain(part, fk.at[0, i])
        push(part, up, hs.at[0, i], hk.at[i])
        part = vo.at[l, :, up]
        drain(part, fv.at[1, i])
        push(part, down, hs.at[1, i], hv.at[i])
    for i in range(8):
        l = loader(i)
        drain(ko.at[l, :, up], fk.at[1, i])
        drain(vo.at[l, :, down], fv.at[0, i])
        drain(ko.at[l, :, far], hk.at[i])
        drain(vo.at[l, :, far], hv.at[i])
        drain(qo.at[l], rq.at[i])
        n = 4 if i else 3
        drain(ko.at[0, pl.ds(0, n), 0], sk.at[i])
        drain(vo.at[0, pl.ds(0, n), 0], sv.at[i])
        drain(qo.at[0, pl.ds(0, n)], sq.at[i])
        for o in range(4):
            drain(ko.at[0, :, 0], fs.at[o, i])
        for o in range(2):
            drain(ko.at[0, :, 0], hs.at[o, i])


def gather(q, k, v):
    dma = pltpu.SemaphoreType.DMA
    any_space = pl.BlockSpec(memory_space=pl.ANY)
    return pl.pallas_call(
        gather_kernel,
        out_shape=(
            jax.ShapeDtypeStruct((8, 4, ROWS, SHARE * D), jnp.bfloat16),
            jax.ShapeDtypeStruct((8, 4, 4, ROWS, D), jnp.bfloat16),
            jax.ShapeDtypeStruct((8, 4, 4, ROWS, D), jnp.bfloat16),
        ),
        in_specs=[any_space] * 3,
        out_specs=[any_space] * 3,
        scratch_shapes=[dma((8,))] * 6 + [dma((2, 8)), dma((2, 8)), dma((4, 8)), dma((8,)), dma((8,)), dma((2, 8))],
        compiler_params=pltpu.CompilerParams(collective_id=0, has_side_effects=True),
    )(q, k, v)


def plan_kernel(seg_ref, tab, cut):
    x, y, z, c = where_am_i()
    labels = seg_ref[pl.ds(x, 1), :]
    s1 = jnp.sum((labels == 0).astype(jnp.int32))
    s2 = s1 + jnp.sum((labels == 1).astype(jnp.int32))
    cut[0], cut[1] = s1, s2

    def tile(t, i):
        t0 = (4 * t + y) * ROWS
        start = jnp.where(t0 >= s2, s2, jnp.where(t0 >= s1, s1, 0))
        k0, k1 = start // B, t0 // B

        def one(kb, i):
            tab[0, i] = t
            tab[1, i] = kb
            tab[2, i] = (kb == k0).astype(jnp.int32)
            tab[3, i] = jnp.where(kb == k1, (t0 - kb * B) // ROWS, NPAT)
            return i + 1

        i = lax.fori_loop(k0, k1 + 1, one, i)
        tab[4, t] = i
        return i

    n = lax.fori_loop(0, TILES, tile, 0)
    cut[2] = n

    def pad(i, _):
        tab[0, i] = 0
        tab[1, i] = 0
        tab[2, i] = 1
        tab[3, i] = NPAT
        return 0

    lax.fori_loop(n, SLOTS + 8, pad, 0)


def plan(seg):
    smem = pl.BlockSpec(memory_space=pltpu.SMEM)
    return pl.pallas_call(
        plan_kernel,
        out_shape=(jax.ShapeDtypeStruct((5, SLOTS + 8), jnp.int32), jax.ShapeDtypeStruct((3,), jnp.int32)),
        in_specs=[pl.BlockSpec(memory_space=pltpu.VMEM)],
        out_specs=(smem, smem),
    )(seg)


def attend_kernel(tab, cut, q_ref, k_ref, v_ref, o_ref, qs, kd, vt, ct, sbuf, pbuf, acc, mref, mc, alr):
    x, y, z, c = where_am_i()
    s1, s2 = cut[0], cut[1]

    def transpose_values(i, _):
        s = pl.multiple_of(i * 512, 512)
        vt[0:D, pl.ds(s, 512)] = v_ref[pl.ds(s, 512), :].T
        vt[D:VR, pl.ds(s, 512)] = jnp.ones((VR - D, 512), jnp.bfloat16)
        u = s + lax.broadcasted_iota(jnp.int32, (512, D), 0)
        r = lax.broadcasted_iota(jnp.int32, (512, D), 1)
        doc = jnp.where(u >= s2, 2, jnp.where(u >= s1, 1, 0)) + ROWS
        kd[pl.ds(s, 512), :] = jnp.where(r == doc, 1.0, 0.0).astype(jnp.bfloat16)
        return 0

    lax.fori_loop(0, SEQ // 512, transpose_values, 0)

    def transpose_queries(t, _):
        s = pl.ds(pl.multiple_of(t * ROWS, ROWS), ROWS)
        tile = jnp.concatenate([q_ref[s, h * D : (h + 1) * D] for h in range(SHARE)], axis=0)
        qs[t, 0:D, :] = tile.T
        row = lax.broadcasted_iota(jnp.int32, (D, L), 1) % ROWS
        dim = lax.broadcasted_iota(jnp.int32, (D, L), 0)
        pos = (4 * t + y) * ROWS + row
        doc = jnp.where(pos >= s2, 2, jnp.where(pos >= s1, 1, 0)) + ROWS
        other = (dim >= ROWS) & (dim < ROWS + 3) & (dim != doc)
        qs[t, D : 2 * D, :] = jnp.where(dim == row, 1.0, jnp.where(other, -BIG, 0.0)).astype(jnp.bfloat16)
        return 0

    lax.fori_loop(0, TILES, transpose_queries, 0)
    u = lax.broadcasted_iota(jnp.int32, (B, D), 0)
    r = lax.broadcasted_iota(jnp.int32, (B, D), 1)
    for p in range(NPAT):
        ct[p] = jnp.where((r < ROWS) & (u > p * ROWS + r), -BIG, 0.0).astype(jnp.bfloat16)
    ct[NPAT] = jnp.zeros((B, D), jnp.bfloat16)
    acc[0] = jnp.zeros((VR, L), jnp.float32)
    mref[...] = jnp.full_like(mref, -BIG)

    def score(i, par):
        t, kb, pattern = tab[0, i], tab[1, i], tab[3, i]
        keys = pl.ds(pl.multiple_of(kb * B, B), B)
        left = jnp.concatenate([k_ref[keys, :], kd[keys, :] + ct[pattern]], axis=1)
        s = jnp.dot(left, qs[t], preferred_element_type=jnp.float32)
        sbuf[par] = s
        mc[par, 0:1, :] = jnp.max(s, axis=0, keepdims=True)

    def weigh(i, par):
        before = jnp.where(tab[2, i] == 1, -1e30, mref[0:1, :])
        top = jnp.maximum(before, mc[par, 0:1, :])
        mref[0:1, :] = top
        alr[par, 0:1, :] = jnp.exp2((before - top) * FACTOR)
        pbuf[par] = jnp.exp2(sbuf[par] * FACTOR - top * FACTOR).astype(jnp.bfloat16)

    def collect(i, par):
        keys = pl.ds(pl.multiple_of(tab[1, i] * B, B), B)
        pv = jnp.dot(vt[:, keys], pbuf[par], preferred_element_type=jnp.float32)
        acc[i + 1] = acc[i] * alr[par, 0:1, :] + pv

    score(0, 0)
    score(1, 1)
    weigh(0, 0)

    def two(j, _):
        for par in range(2):
            i = 2 * j + par
            collect(i, par)
            weigh(i + 1, 1 - par)
            score(i + 2, par)
        return 0

    lax.fori_loop(0, (cut[2] + 1) // 2, two, 0)

    def finish(t, _):
        i = tab[4, t]
        a = acc[i, 0:D, :] / acc[i, D : D + 1, :]
        at = a.T.astype(jnp.bfloat16)
        for h in range(SHARE):
            s = pl.ds(pl.multiple_of(t * ROWS, ROWS), ROWS)
            o_ref[s, h * D : (h + 1) * D] = at[h * ROWS : (h + 1) * ROWS, :]
        return 0

    lax.fori_loop(0, TILES, finish, 0)


def attend(tab, cut, q, k, v):
    smem, vmem = pl.BlockSpec(memory_space=pltpu.SMEM), pl.BlockSpec(memory_space=pltpu.VMEM)
    return pl.pallas_call(
        attend_kernel,
        out_shape=jax.ShapeDtypeStruct((TILES * ROWS, SHARE * D), jnp.bfloat16),
        in_specs=[smem, smem, vmem, vmem, vmem],
        out_specs=vmem,
        scratch_shapes=[
            pltpu.VMEM((TILES, 2 * D, L), jnp.bfloat16),
            pltpu.VMEM((SEQ, D), jnp.bfloat16),
            pltpu.VMEM((VR, SEQ), jnp.bfloat16),
            pltpu.VMEM((NPAT + 1, B, D), jnp.bfloat16),
            pltpu.VMEM((2, B, L), jnp.float32),
            pltpu.VMEM((2, B, L), jnp.bfloat16),
            pltpu.VMEM((SLOTS + 2, VR, L), jnp.float32),
            pltpu.VMEM((8, L), jnp.float32),
            pltpu.VMEM((2, 8, L), jnp.float32),
            pltpu.VMEM((2, 8, L), jnp.float32),
        ],
        compiler_params=pltpu.CompilerParams(vmem_limit_bytes=60 * 2**20),
    )(tab, cut, q.reshape(TILES * ROWS, SHARE * D), k.reshape(SEQ, D), v.reshape(SEQ, D))


def return_kernel(o_ref, out_ref, send, recv):
    x, y, z, c = where_am_i()
    greet(x, y, z, c, False)
    cols = pl.ds(pl.multiple_of((z * 2 + c) * SHARE * D, 128), SHARE * D)
    dst = out_ref.at[0, x, :, cols]
    for dx in range(4):
        for dc in range(2):
            for dz in range(4):
                l, z2 = ((x + dx) % 4) * 2 + (c + dc) % 2, (z + dz) % 4
                src = o_ref.at[l, z2]
                if dx or dc or dz:
                    pltpu.make_async_remote_copy(
                        src_ref=src,
                        dst_ref=dst,
                        send_sem=send.at[dx],
                        recv_sem=recv,
                        device_id=(z2 * 4 + y, l),
                        device_id_type=MESH,
                    ).start()
                else:
                    pltpu.make_async_copy(src, dst, recv).start()
    drain(out_ref, recv)
    for dx in range(4):
        drain(out_ref.at[0, 0, :, pl.ds(0, (8 if dx else 7) * SHARE * D)], send.at[dx])


def give_back(o):
    dma = pltpu.SemaphoreType.DMA
    any_space = pl.BlockSpec(memory_space=pl.ANY)
    return pl.pallas_call(
        return_kernel,
        out_shape=jax.ShapeDtypeStruct((1, 4, ROWS, 4096), jnp.bfloat16),
        in_specs=[any_space],
        out_specs=any_space,
        scratch_shapes=[dma((4,)), dma(())],
        compiler_params=pltpu.CompilerParams(collective_id=1, has_side_effects=True),
    )(o)


def per_device(query_rows, key_rows, value_rows, segment_ids):
    tab, cut = plan(segment_ids)
    q, k, v = gather(query_rows, key_rows, value_rows)
    out = attend(tab, cut, q, k, v)
    return give_back(out.reshape(8, 4, ROWS, SHARE * D))


def solution(mesh):
    return jax.shard_map(
        per_device,
        mesh=mesh,
        in_specs=(
            P("dp", None, "grp", None),
            P("dp", None, "grp", None),
            P("dp", None, "grp", None),
            P(),
        ),
        out_specs=P("dp", None, "grp", None),
        check_vma=False,
    )
```

time: 790 us -> 147 us (0.19)
  matrix products: 404 us -> 0 us
  local copies, waits for them, and re-layouts: 168 us -> 3.13 us
  Pallas kernels: 0 us -> 144 us
  waiting for transfers between devices: 76.3 us -> 0 us
  blocking collectives: 61.9 us -> 0 us
  starting transfers between devices: 38.9 us -> 0 us
  loops' own time: 29.1 us -> 0 us
    dot_general x408 -> x0, matrix products: 404 us -> none  [the longest x272 367 us: key_scores(): jnp.einsum('qhd,khd->hqk', query_block, key_block, preferred_element_type...]
    pallas_call x0 -> x4, Pallas kernels: none -> 144 us  [the longest x1 55.1 us: gather(): pl.pallas_call(gather_kernel, out_shape=(jax.ShapeDtypeStruct((8, 4, ROWS...]
    all_to_all x6 -> x0, waiting for transfers between devices: 76.3 us -> none  [the longest x1 26.3 us: per_device(): lax.all_to_all(lax.all_to_all(halves_first(value_wide), 'grp', split_axis...]
    all_to_all x2 -> x0, blocking collectives: 61.9 us -> none  [the longest x1 31.9 us: per_device(): lax.all_to_all(lax.all_to_all(shaped, 'grp', split_axis=2, concat_axis=3,...]
    dynamic_slice x321 -> x0, local copies, waits for them, and re-layouts: 46.7 us -> none  [the longest x272 21.5 us: key_scores(): key_labels = lax.dynamic_slice_in_dim(labels, key_start, block, 0)]
    unnamed x16 -> x1, local copies, waits for them, and re-layouts: 42.6 us -> 3.13 us
    all_to_all x6 -> x0, starting transfers between devices: 38.9 us -> none  [the longest x1 9.29 us: per_device(): lax.all_to_all(lax.all_to_all(halves_first(query_rows), 'grp', split_axis...]
    another operation x33 -> x0, loops' own time: 29.1 us -> none  [the longest x1 19.1 us: attend(): blocks = lax.map(one_block, jnp.arange(seq_len // block, dtype=jnp.int32))]
  transfers between devices with their start and end apart: 6 -> 0, of which waited for: 6 -> 0; matrix products, arithmetic and copies ran while one was open for 11% -> 0% of each run, Pallas kernels for 0% -> 0%
where the time goes in v1:
time: 147 us
  Pallas kernels  144 us (98%)
  local copies, waits for them, and re-layouts  3.13 us (2%)
    pallas_call x1, Pallas kernels, gather(): pl.pallas_call(gather_kernel, out_shape=(jax.ShapeDtypeStruct((8, 4, ROWS...  55.1 us
    pallas_call x1, Pallas kernels, attend(): pl.pallas_call(attend_kernel, out_shape=jax.ShapeDtypeStruct((TILES * ROW...  50.5 us
    pallas_call x1, Pallas kernels, give_back(): pl.pallas_call(return_kernel, out_shape=jax.ShapeDtypeStruct((1, 4, ROWS,...  33.5 us
    pallas_call x1, Pallas kernels, plan(): pl.pallas_call(plan_kernel, out_shape=(jax.ShapeDtypeStruct((5, SLOTS + 8...  4.97 us
    unnamed x1, local copies, waits for them, and re-layouts  3.13 us

profile of v1, /device:TPU:1, one launch (start us, length us, event | category | flops | bytes accessed | tf_op | source)
XLA Modules:
  0.0 147.2 jit_solution(13322777089112699188)
XLA Ops:
  0.0 5.0 %shard_map.46 = (s32[5,200]{1,0:T(8,128)}, s32[3]{0:T(128)}) custom-call(s32[4,8192]{1,0:T(4,128)} %seg_ref.1), custom_call_target="tpu_custom_call" | custom-call | tf_op jit(solution)/shard_map/pallas_call | solution.py:202
  5.0 55.1 %shard_map.47 = (bf16[8,4,64,512]{3,2,1,0:T(8,128)(2,1)}, bf16[8,4,4,64,128]{4,3,2,1,0:T(8,128)(2,1)}, bf16[8,4,4,64,128]{4,3,2,1,0:T(8,128)(2,1)}) custom-call(bf16[1,4,64,4096]{3,2,1,0:T(8,128)(2,1)} %q_ref.1, bf16[1,4,64,1024]{3,2,1,0:T(8,128)(2,1)} %k_ref.1, bf16[1,4,64,1024]{3,2,1,0:T(8,128)(2,1)} %v_ref.1), custom_call_target="tpu_custom_call" | custom-call | tf_op jit(solution)/shard_map/pallas_call | solution.py:150
  60.1 50.5 %shard_map.48 = bf16[2048,512]{1,0:T(8,128)(2,1)} custom-call(s32[5,200]{1,0:T(8,128)} %get-tuple-element.10.tab, s32[3]{0:T(128)} %get-tuple-element.11.cut, bf16[2048,512]{1,0:T(8,128)(2,1)} %bitcast.5, bf16[8192,128]{1,0:T(8,128)(2,1)} %bitcast.6, bf16[8192,128]{1,0:T(8,128)(2,1)} %bitcast.7), custom_call_target="tpu_custom_call" | custom-call | tf_op jit(solution)/shard_map/pallas_call | solution.py:295
  110.6 33.5 %shard_map.49 = bf16[1,4,64,4096]{3,2,1,0:T(8,128)(2,1)} custom-call(bf16[8,4,64,512]{3,2,1,0:T(8,128)(2,1)} %bitcast.4), custom_call_target="tpu_custom_call" | custom-call | tf_op jit(solution)/shard_map/pallas_call | solution.py:345
  144.1 3.1 %copy.6 = bf16[1,4,64,4096]{3,2,1,0:T(8,128)(2,1)} copy(bf16[1,4,64,4096]{3,2,1,0:T(8,128)(2,1)} %shard_map.49) | data formatting | bytes 4194304

commit v2 on v0

v2 whole, which is shorter than its diff:
```python
import math

import jax
import jax.numpy as jnp
import numpy as np
from jax import lax
from jax.experimental import pallas as pl
from jax.experimental.pallas import tpu as pltpu
from jax.sharding import PartitionSpec as P

MESH = pl.DeviceIdType.MESH
SEQ = 8192
ROWS = 64
SHARE = 4
D = 128
L = SHARE * ROWS
TILES = 32
B = 512
VR = D + 16
BIG = float(2**20)
LONGEST = 5461
FACTOR = float(np.log2(np.e) / math.sqrt(D))
BF16 = jnp.bfloat16


def phase_steps():
    worst = [0] * 4
    cuts = np.arange(0, SEQ, ROWS) + 1
    s1, s2 = np.meshgrid(cuts, cuts, indexing="ij")
    slack = LONGEST + ROWS
    fits = (s2 >= s1) & (s1 <= slack) & (s2 - s1 <= slack) & (SEQ - s2 <= slack)
    s1, s2 = s1[fits], s2[fits]
    for phase in range(4):
        zz, u = phase // 2, phase % 2
        for c in range(2):
            for low in range(2):
                count = np.zeros(s1.shape, int)
                for l in range(8):
                    t0 = l * 1024 + (c + 2 * zz) * 256 + (3 - low if u else low) * ROWS
                    start = np.where(t0 >= s2, s2, np.where(t0 >= s1, s1, 0))
                    count += t0 // B - start // B + 1
                worst[phase] = max(worst[phase], int(count.max()))
    return [n + n % 2 for n in worst]


STEPS = phase_steps()
SLOTS = max(STEPS) + 2


def drain(ref, sem):
    pltpu.make_async_copy(ref, ref, sem).wait()


def kernel(
    seg_ref, q_ref, k_ref, v_ref, out_ref, qbuf, kbuf, vbuf, qs, kd, vt, ct, sbuf, pbuf, acc, mref, mc, alr, obuf, last,
    s_kv, r_kv, s_q, r_q, s_sib, r_sib, s_par, r_par, s_hop, r_hop, s_out, r_out,
):
    gi, di = lax.axis_index("grp"), lax.axis_index("dp")
    x, y, z, c = di // 2, gi % 4, gi // 4, di % 2
    half = y // 2
    low = jnp.minimum(y, 3 - y)
    up = (y > 1).astype(jnp.int32)
    mate = y + 1 - 2 * (y % 2)
    core = z % 2
    mine = core == c
    sibling = (gi, x * 2 + 1 - c)
    partner = (z * 4 + mate, di)

    barrier = pltpu.get_barrier_semaphore()
    n = 0
    for dx in range(4):
        for dz in range(4):
            for dh in range(2):
                for dc in range(2):
                    if dx or dz or dh or dc:
                        to = (((z + dz) % 4) * 4 + (3 - y if dh else y), ((x + dx) % 4) * 2 + (c + dc) % 2)
                        pl.semaphore_signal(barrier, inc=1, device_id=to, device_id_type=MESH)
                        n += 1
    pl.semaphore_signal(barrier, inc=1, device_id=partner, device_id_type=MESH)
    pl.semaphore_wait(barrier, n + 1)

    def remote(src, dst, send, recv, to):
        pltpu.make_async_remote_copy(
            src_ref=src, dst_ref=dst, send_sem=send, recv_sem=recv, device_id=to, device_id_type=MESH
        ).start()

    def spread(pairs, width, send, recv):
        for dx in range(4):
            for dz in range(4):
                for dh in range(2):
                    g, z2 = (x + dx) % 4, (z + dz) % 4
                    h2, y2 = (1 - half, 3 - y) if dh else (half, y)
                    cols = pl.ds(pl.multiple_of((z2 * 2 + h2) * width, 128), width)
                    to = (z2 * 4 + y2, g * 2 + core)
                    for src, dst in pairs:
                        piece = src.at[0, g, :, cols]
                        if dx or dz or dh:
                            remote(piece, dst, send.at[dx], recv.at[di], to)
                        else:

                            @pl.when(mine)
                            def _():
                                pltpu.make_async_copy(piece, dst, recv.at[di]).start()

                            @pl.when(jnp.logical_not(mine))
                            def _():
                                remote(piece, dst, send.at[dx], recv.at[di], to)

    here = (di * 2 + z // 2, core, low, up)
    spread(((k_ref, kbuf.at[here]), (v_ref, vbuf.at[here])), D, s_kv, r_kv)
    spread(((q_ref, qbuf.at[di, z // 2, up]),), SHARE * D, s_q, r_q)

    labels = seg_ref[pl.ds(x, 1), :]
    s1 = jnp.sum((labels == 0).astype(jnp.int32))
    s2 = s1 + jnp.sum((labels == 1).astype(jnp.int32))

    def document(pos):
        return jnp.where(pos >= s2, 2, jnp.where(pos >= s1, 1, 0))

    u = lax.broadcasted_iota(jnp.int32, (B, D), 0)
    r = lax.broadcasted_iota(jnp.int32, (B, D), 1)
    slot = (u // ROWS) % 4
    place = (u // 256) * 256 + u % ROWS + jnp.where(slot % 2 == 1, 3 - slot // 2, slot // 2) * ROWS

    def key_documents(kb, _):
        kd[kb] = jnp.where(r == document(place + kb * B) + ROWS, 1.0, 0.0).astype(BF16)
        vt[kb, D:VR, :] = jnp.ones((VR - D, B), BF16)
        return 0

    lax.fori_loop(0, SEQ // B, key_documents, 0)
    for side in range(2):
        mine_y = 3 - low if side else low
        ct[side] = jnp.where((r < ROWS) & (place > c * 256 + mine_y * ROWS + r), -BIG, 0.0).astype(BF16)
    ct[2] = jnp.zeros((B, D), BF16)
    row = lax.broadcasted_iota(jnp.int32, (D, L), 1) % ROWS
    dim = lax.broadcasted_iota(jnp.int32, (D, L), 0)

    def block_start(l, zz, side):
        return l * 1024 + (c + 2 * zz) * 256 + (3 - low if side else low) * ROWS

    def query_documents(l, _):
        for zz in range(2):
            for side in range(2):
                doc = document(block_start(l, zz, side) + row) + ROWS
                other = (dim >= ROWS) & (dim < ROWS + 3) & (dim != doc)
                value = jnp.where(dim == row, 1.0, jnp.where(other, -BIG, 0.0))
                qs[(l * 2 + zz) * 2 + side, D : 2 * D, :] = value.astype(BF16)
        return 0

    lax.fori_loop(0, 8, query_documents, 0)
    acc[0] = jnp.zeros((VR, L), jnp.float32)
    mref[...] = jnp.full_like(mref, -BIG)

    def loader(i):
        return ((x + 4 - i // 2) % 4) * 2 + (c + i % 2) % 2

    for i in range(8):
        l = loader(i)
        drain(kbuf.at[0], r_kv.at[l])
        for buf in (kbuf, vbuf):
            part = buf.at[pl.ds(2 * l, 2), c, low]
            remote(part, part, s_sib.at[i], r_sib.at[l], sibling)
            remote(part, part, s_par.at[i], r_par.at[l], partner)
    theirs = jnp.minimum(mate, 3 - mate)
    for i in range(8):
        l = loader(i)
        drain(kbuf.at[0], r_par.at[l])
        for buf in (kbuf, vbuf):
            part = buf.at[pl.ds(2 * l, 2), c, theirs]
            remote(part, part, s_hop.at[i], r_hop.at[l], sibling)

    def turn_queries(l, _):
        drain(qbuf.at[0], r_q.at[l])
        for zz in range(2):
            for side in range(2):
                t = (l * 2 + zz) * 2 + side
                tile = jnp.concatenate([qbuf[l, zz, side, :, h * D : (h + 1) * D] for h in range(SHARE)], axis=0)
                qs[t, 0:D, :] = tile.T
        return 0

    lax.fori_loop(0, 8, turn_queries, 0)

    def turn_values(l, _):
        drain(kbuf.at[0], r_sib.at[l])
        drain(kbuf.at[0], r_hop.at[l])
        for zz in range(2):
            vt[2 * l + zz, 0:D, :] = vbuf[2 * l + zz].reshape(B, D).T
        return 0

    lax.fori_loop(0, 8, turn_values, 0)

    head = z * 2 + half
    result = out_ref.at[0, x, :, pl.ds(pl.multiple_of(head * SHARE * D, 128), SHARE * D)]

    for phase in range(4):
        zz, side = phase // 2, phase % 2

        def first_block(l):
            t0 = block_start(l, zz, side)
            return jnp.where(t0 >= s2, s2, jnp.where(t0 >= s1, s1, 0)) // B

        def advance(l, kb):
            done = kb >= 2 * l + zz
            l2 = jnp.where(done, jnp.minimum(l + 1, 7), l)
            return l2, jnp.where(done, first_block(l2), kb + 1)

        def score(l, kb, par):
            mask = ct[jnp.where(kb == 2 * l + zz, side, 2)]
            left = jnp.concatenate([kbuf[kb].reshape(B, D), kd[kb] + mask], axis=1)
            s = jnp.dot(left, qs[(l * 2 + zz) * 2 + side], preferred_element_type=jnp.float32)
            sbuf[par] = s
            mc[par, 0:1, :] = jnp.max(s, axis=0, keepdims=True)

        def weigh(first, par):
            before = jnp.where(first == 1, -1e30, mref[0:1, :])
            top = jnp.maximum(before, mc[par, 0:1, :])
            mref[0:1, :] = top
            alr[par, 0:1, :] = jnp.exp2((before - top) * FACTOR)
            pbuf[par] = jnp.exp2(sbuf[par] * FACTOR - top * FACTOR).astype(BF16)

        def collect(i, kb, par):
            pv = jnp.dot(vt[kb], pbuf[par], preferred_element_type=jnp.float32)
            acc[i + 1] = acc[i] * alr[par, 0:1, :] + pv

        def opens(l, kb):
            return (kb == first_block(l)).astype(jnp.int32)

        l0 = jnp.int32(0)
        b0 = first_block(l0)
        l1, b1 = advance(l0, b0)
        score(l0, b0, 0)
        score(l1, b1, 1)
        weigh(jnp.int32(1), 0)

        def two(j, carry):
            b0, b1, f1, l1 = carry
            for par in range(2):
                collect(2 * j + par, b0, par)
                weigh(f1, 1 - par)
                l2, b2 = advance(l1, b1)
                score(l2, b2, par)
                b0, b1, f1, l1 = b1, b2, opens(l2, b2), l2
            return b0, b1, f1, l1

        lax.fori_loop(0, STEPS[phase] // 2, two, (b0, b1, opens(l1, b1), l1))

        def count(l, done):
            done = done + 2 * l + zz - first_block(l) + 1
            last[l] = jnp.minimum(done, STEPS[phase])
            return done

        lax.fori_loop(0, 8, count, jnp.int32(0))

        def finish(j, _):
            l = (di + j) % 8
            i = last[l]
            a = acc[i, 0:D, :] / acc[i, D : D + 1, :]
            at = a.T.astype(BF16)
            tile = obuf.at[l, zz, side]
            for h in range(SHARE):
                obuf[l, zz, side, :, h * D : (h + 1) * D] = at[h * ROWS : (h + 1) * ROWS, :]
            to_z, to_y = c + 2 * zz, 3 - low if side else low
            own = (l == di) & (to_z == z) & (to_y == y)

            @pl.when(own)
            def _():
                pltpu.make_async_copy(tile, result, r_out).start()

            @pl.when(jnp.logical_not(own))
            def _():
                remote(tile, result, s_out.at[l, phase], r_out, (to_z * 4 + to_y, l))

            return 0

        lax.fori_loop(0, 8, finish, 0)

    drain(out_ref, r_out)
    for dx in range(4):
        if dx:
            drain(kbuf.at[pl.ds(0, 2)], s_kv.at[dx])
            drain(qbuf.at[pl.ds(0, 2)], s_q.at[dx])
        else:

            @pl.when(mine)
            def _():
                drain(kbuf.at[pl.ds(0, 7), :, 0, 0], s_kv.at[dx])
                drain(qbuf.at[pl.ds(0, 7), 0, 0], s_q.at[dx])

            @pl.when(jnp.logical_not(mine))
            def _():
                drain(kbuf.at[pl.ds(0, 2)], s_kv.at[dx])
                drain(qbuf.at[pl.ds(0, 2)], s_q.at[dx])

    def sent(i, _):
        for sem in (s_sib, s_par, s_hop):
            drain(kbuf.at[0], sem.at[i])
        for phase in range(4):
            zz, side = phase // 2, phase % 2
            to_z, to_y = c + 2 * zz, 3 - low if side else low

            @pl.when(jnp.logical_not((i == di) & (to_z == z) & (to_y == y)))
            def _():
                drain(obuf.at[0, 0, 0], s_out.at[i, phase])

        return 0

    lax.fori_loop(0, 8, sent, 0)


def per_device(query_rows, key_rows, value_rows, segment_ids):
    dma = pltpu.SemaphoreType.DMA
    vmem = pltpu.VMEM
    any_space = pl.BlockSpec(memory_space=pl.ANY)
    return pl.pallas_call(
        kernel,
        out_shape=jax.ShapeDtypeStruct((1, 4, ROWS, 4096), BF16),
        in_specs=[pl.BlockSpec(memory_space=vmem)] + [any_space] * 3,
        out_specs=any_space,
        scratch_shapes=[
            vmem((8, 2, 2, ROWS, SHARE * D), BF16),
            vmem((16, 2, 2, 2, ROWS, D), BF16),
            vmem((16, 2, 2, 2, ROWS, D), BF16),
            vmem((TILES, 2 * D, L), BF16),
            vmem((16, B, D), BF16),
            vmem((16, VR, B), BF16),
            vmem((3, B, D), BF16),
            vmem((2, B, L), jnp.float32),
            vmem((2, B, L), BF16),
            vmem((SLOTS, VR, L), jnp.float32),
            vmem((8, L), jnp.float32),
            vmem((2, 8, L), jnp.float32),
            vmem((2, 8, L), jnp.float32),
            vmem((8, 2, 2, ROWS, SHARE * D), BF16),
            pltpu.SMEM((8,), jnp.int32),
            dma((4,)), dma((8,)), dma((4,)), dma((8,)), dma((8,)), dma((8,)),
            dma((8,)), dma((8,)), dma((8,)), dma((8,)), dma((8, 4)), dma(()),
        ],
        compiler_params=pltpu.CompilerParams(
            collective_id=0, has_side_effects=True, vmem_limit_bytes=60 * 2**20
        ),
    )(segment_ids, query_rows, key_rows, value_rows)


def solution(mesh):
    return jax.shard_map(
        per_device,
        mesh=mesh,
        in_specs=(
            P("dp", None, "grp", None),
            P("dp", None, "grp", None),
            P("dp", None, "grp", None),
            P(),
        ),
        out_specs=P("dp", None, "grp", None),
        check_vma=False,
    )
```

time: 790 us -> 124 us (0.16)
  the two profiles are of different devices: /device:TPU:1 before, /device:TPU:89 now
where the time goes in v2:
time: 124 us
  Pallas kernels  121 us (98%)
  local copies, waits for them, and re-layouts  3.13 us (3%)
    pallas_call x1, Pallas kernels, per_device(): pl.pallas_call(kernel, out_shape=jax.ShapeDtypeStruct((1, 4, ROWS, 4096),...  121 us
    unnamed x1, local copies, waits for them, and re-layouts  3.13 us

profile of v2, /device:TPU:89, one launch (start us, length us, event | category | flops | bytes accessed | tf_op | source)
XLA Modules:
  0.0 123.9 jit_solution(7206762503933812898)
XLA Ops:
  0.0 120.8 %shard_map.46 = bf16[1,4,64,4096]{3,2,1,0:T(8,128)(2,1)} custom-call(s32[4,8192]{1,0:T(4,128)} %seg_ref.1, bf16[1,4,64,4096]{3,2,1,0:T(8,128)(2,1)} %q_ref.1, bf16[1,4,64,1024]{3,2,1,0:T(8,128)(2,1)} %k_ref.1, bf16[1,4,64,1024]{3,2,1,0:T(8,128)(2,1)} %v_ref.1), custom_call_target="tpu_custom_call" | custom-call | tf_op jit(solution)/shard_map/pallas_call | solution.py:314
  120.8 3.1 %copy.6 = bf16[1,4,64,4096]{3,2,1,0:T(8,128)(2,1)} copy(bf16[1,4,64,4096]{3,2,1,0:T(8,128)(2,1)} %shard_map.46) | data formatting | bytes 4194304

commit v3 on v2

v3 whole, which is shorter than its diff:
```python
import math

import jax
import jax.numpy as jnp
import numpy as np
from jax import lax
from jax.experimental import pallas as pl
from jax.experimental.pallas import tpu as pltpu
from jax.sharding import PartitionSpec as P

MESH = pl.DeviceIdType.MESH
SEQ = 8192
ROWS = 64
SHARE = 4
D = 128
L = SHARE * ROWS
TILES = 32
B = 512
VR = D + 16
BIG = float(2**20)
LONGEST = 5461
FACTOR = float(np.log2(np.e) / math.sqrt(D))
BF16 = jnp.bfloat16


def phase_steps():
    worst = [0] * 2
    cuts = np.arange(0, SEQ, ROWS) + 1
    s1, s2 = np.meshgrid(cuts, cuts, indexing="ij")
    slack = LONGEST + ROWS
    fits = (s2 >= s1) & (s1 <= slack) & (s2 - s1 <= slack) & (SEQ - s2 <= slack)
    s1, s2 = s1[fits], s2[fits]
    for zz in range(2):
        for c in range(2):
            for y in range(4):
                count = np.zeros(s1.shape, int)
                for l in range(8):
                    t0 = l * 1024 + (c + 2 * zz) * 256 + y * ROWS
                    start = np.where(t0 >= s2, s2, np.where(t0 >= s1, s1, 0))
                    count += t0 // B - start // B + 1
                worst[zz] = max(worst[zz], int(count.max()))
    return [n + n % 2 for n in worst]


STEPS = phase_steps()
SLOTS = max(STEPS) + 2


def drain(ref, sem):
    pltpu.make_async_copy(ref, ref, sem).wait()


def kernel(
    seg_ref, q_ref, k_ref, v_ref, out_ref, qbuf, kva, kvb, qs, qd, kd, vt, ct, sbuf, pbuf, acc, mref, mc, alr, obuf, last,
    s_kv, r_kv, s_q, r_q, s_f, r_f, s_r, r_r, r_s, s_out, r_out,
):
    gi, di = lax.axis_index("grp"), lax.axis_index("dp")
    x, y, z, c = di // 2, gi % 4, gi // 4, di % 2
    core = z % 2
    mine = core == c
    other_core = (gi, x * 2 + 1 - c)
    up, down, far = (y + 1) % 4, (y + 3) % 4, (y + 2) % 4
    up_chip, down_chip = (z * 4 + up, di), (z * 4 + down, di)
    kvs = (kva, kvb)

    barrier = pltpu.get_barrier_semaphore()
    n = 0
    for dx in range(4):
        for dz in range(4):
            for dc in range(2):
                if dx or dz or dc:
                    to = (((z + dz) % 4) * 4 + y, ((x + dx) % 4) * 2 + (c + dc) % 2)
                    pl.semaphore_signal(barrier, inc=1, device_id=to, device_id_type=MESH)
                    n += 1
    for to in (up_chip, down_chip):
        pl.semaphore_signal(barrier, inc=1, device_id=to, device_id_type=MESH)
        n += 1
    pl.semaphore_wait(barrier, n)

    def remote(src, dst, send, recv, to):
        pltpu.make_async_remote_copy(
            src_ref=src, dst_ref=dst, send_sem=send, recv_sem=recv, device_id=to, device_id_type=MESH
        ).start()

    def spread(pairs, h, width, send, recv):
        for dx in range(4):
            for dz in range(4):
                g, z2 = (x + dx) % 4, (z + dz) % 4
                cols = pl.ds(pl.multiple_of((z2 * 2 + h) * width, 128), width)
                to = (z2 * 4 + y, g * 2 + core)
                for src, dst in pairs:
                    piece = src.at[0, g, :, cols]
                    if dx or dz:
                        remote(piece, dst, send.at[h, dx], recv.at[h, x], to)
                    else:

                        @pl.when(mine)
                        def _():
                            pltpu.make_async_copy(piece, dst, recv.at[h, x]).start()

                        @pl.when(jnp.logical_not(mine))
                        def _():
                            remote(piece, dst, send.at[h, dx], recv.at[h, x], to)

    def spread_head(h):
        block = di * 2 + z // 2
        spread(((k_ref, kvs[h].at[block, core, y, 0]), (v_ref, kvs[h].at[block, core, y, 1])), h, D, s_kv, r_kv)
        spread(((q_ref, qbuf.at[h, di, z // 2]),), h, SHARE * D, s_q, r_q)

    whole, part_of_one = kva.at[0, 0], kva.at[0, 0, :, 0]

    def source(i):
        return (x + 4 - i) % 4

    def part(h, xs, whose):
        return kvs[h].at[pl.ds(4 * xs, 4), c, whose]

    def forward(h):
        for i in range(4):
            xs = source(i)
            drain(whole, r_kv.at[h, xs])
            own = part(h, xs, y)
            remote(own, own, s_f.at[h, 0, i], r_f.at[h, 0, xs], up_chip)
            remote(own, own, s_f.at[h, 1, i], r_f.at[h, 1, xs], down_chip)
            remote(own, own, s_f.at[h, 2, i], r_s.at[h, 0, xs], other_core)

    def relay(h):
        for i in range(4):
            xs = source(i)
            drain(whole, r_f.at[h, 0, xs])
            keys = kvs[h].at[pl.ds(4 * xs, 4), c, down, 0]
            remote(keys, keys, s_r.at[h, 0, i], r_r.at[h, 0, xs], up_chip)
            drain(whole, r_f.at[h, 1, xs])
            values = kvs[h].at[pl.ds(4 * xs, 4), c, up, 1]
            remote(values, values, s_r.at[h, 1, i], r_r.at[h, 1, xs], down_chip)
            remote(part(h, xs, down), part(h, xs, down), s_r.at[h, 2, i], r_s.at[h, 1, xs], other_core)
            remote(part(h, xs, up), part(h, xs, up), s_r.at[h, 3, i], r_s.at[h, 2, xs], other_core)

    def complete(h):
        for i in range(4):
            xs = source(i)
            drain(part_of_one, r_r.at[h, 0, xs])
            drain(part_of_one, r_r.at[h, 1, xs])
            remote(part(h, xs, far), part(h, xs, far), s_r.at[h, 4, i], r_s.at[h, 3, xs], other_core)

    spread_head(0)

    labels = seg_ref[pl.ds(x, 1), :]
    s1 = jnp.sum((labels == 0).astype(jnp.int32))
    s2 = s1 + jnp.sum((labels == 1).astype(jnp.int32))

    def document(pos):
        return jnp.where(pos >= s2, 2, jnp.where(pos >= s1, 1, 0))

    u = lax.broadcasted_iota(jnp.int32, (B, D), 0)
    r = lax.broadcasted_iota(jnp.int32, (B, D), 1)

    def key_documents(kb, _):
        kd[kb] = jnp.where(r == document(u + kb * B) + ROWS, 1.0, 0.0).astype(BF16)
        vt[kb, D:VR, :] = jnp.ones((VR - D, B), BF16)
        return 0

    lax.fori_loop(0, SEQ // B, key_documents, 0)
    ct[0] = jnp.where((r < ROWS) & (u > c * 256 + y * ROWS + r), -BIG, 0.0).astype(BF16)
    ct[1] = jnp.zeros((B, D), BF16)
    row = lax.broadcasted_iota(jnp.int32, (D, L), 1) % ROWS
    dim = lax.broadcasted_iota(jnp.int32, (D, L), 0)

    def query_documents(kb, _):
        doc = document(kb * B + c * 256 + y * ROWS + row) + ROWS
        other = (dim >= ROWS) & (dim < ROWS + 3) & (dim != doc)
        qd[kb] = jnp.where(dim == row, 1.0, jnp.where(other, -BIG, 0.0)).astype(BF16)
        return 0

    lax.fori_loop(0, SEQ // B, query_documents, 0)
    acc[0] = jnp.zeros((VR, L), jnp.float32)
    mref[...] = jnp.full_like(mref, -BIG)

    def prepare(h):
        def turn_queries(xs, _):
            drain(qbuf.at[0, pl.ds(0, 2)], r_q.at[h, xs])
            for t in range(4):
                l, zz = 2 * xs + t // 2, t % 2
                tile = jnp.concatenate([qbuf[h, l, zz, :, j * D : (j + 1) * D] for j in range(SHARE)], axis=0)
                qs[h * 16 + 4 * xs + t] = tile.T
            return 0

        lax.fori_loop(0, 4, turn_queries, 0)

        def turn_values(xs, _):
            for o in range(4):
                drain(whole, r_s.at[h, o, xs])
            for t in range(4):
                vt[4 * xs + t, 0:D, :] = kvs[h][4 * xs + t, :, :, 1].reshape(B, D).T
            return 0

        lax.fori_loop(0, 4, turn_values, 0)

    def work(h, zz, between):
        kv = kvs[h]

        def first_block(l):
            t0 = l * 1024 + (c + 2 * zz) * 256 + y * ROWS
            return jnp.where(t0 >= s2, s2, jnp.where(t0 >= s1, s1, 0)) // B

        def advance(l, kb):
            done = kb >= 2 * l + zz
            l2 = jnp.where(done, jnp.minimum(l + 1, 7), l)
            return l2, jnp.where(done, first_block(l2), kb + 1)

        def score(l, kb, par):
            mask = ct[jnp.where(kb == 2 * l + zz, 0, 1)]
            left = jnp.concatenate([kv[kb, :, :, 0].reshape(B, D), kd[kb] + mask], axis=1)
            right = jnp.concatenate([qs[h * 16 + 2 * l + zz], qd[2 * l + zz]], axis=0)
            s = jnp.dot(left, right, preferred_element_type=jnp.float32)
            sbuf[par] = s
            mc[par, 0:1, :] = jnp.max(s, axis=0, keepdims=True)

        def weigh(first, par):
            before = jnp.where(first == 1, -1e30, mref[0:1, :])
            top = jnp.maximum(before, mc[par, 0:1, :])
            mref[0:1, :] = top
            alr[par, 0:1, :] = jnp.exp2((before - top) * FACTOR)
            pbuf[par] = jnp.exp2(sbuf[par] * FACTOR - top * FACTOR).astype(BF16)

        def collect(i, kb, par):
            pv = jnp.dot(vt[kb], pbuf[par], preferred_element_type=jnp.float32)
            acc[i + 1] = acc[i] * alr[par, 0:1, :] + pv

        def opens(l, kb):
            return (kb == first_block(l)).astype(jnp.int32)

        l0 = jnp.int32(0)
        b0 = first_block(l0)
        l1, b1 = advance(l0, b0)
        score(l0, b0, 0)
        score(l1, b1, 1)
        weigh(jnp.int32(1), 0)

        def two(j, carry):
            b0, b1, f1, l1 = carry
            for par in range(2):
                collect(2 * j + par, b0, par)
                weigh(f1, 1 - par)
                l2, b2 = advance(l1, b1)
                score(l2, b2, par)
                b0, b1, f1, l1 = b1, b2, opens(l2, b2), l2
            return b0, b1, f1, l1

        carry = (b0, b1, opens(l1, b1), l1)
        pairs = STEPS[zz] // 2
        if between is None:
            lax.fori_loop(0, pairs, two, carry)
        else:
            carry = lax.fori_loop(0, pairs // 2, two, carry)
            between(h + 1)
            lax.fori_loop(pairs // 2, pairs, two, carry)

        def count(l, done):
            done = done + 2 * l + zz - first_block(l) + 1
            last[l] = jnp.minimum(done, STEPS[zz])
            return done

        lax.fori_loop(0, 8, count, jnp.int32(0))
        to_z = c + 2 * zz
        cols = pl.ds(pl.multiple_of((z * 2 + h) * SHARE * D, 128), SHARE * D)

        def finish(j, _):
            l = (di + j) % 8
            i = last[l]
            a = acc[i, 0:D, :] / acc[i, D : D + 1, :]
            at = a.T.astype(BF16)
            tile = obuf.at[h, l, zz]
            for o in range(SHARE):
                obuf[h, l, zz, :, o * D : (o + 1) * D] = at[o * ROWS : (o + 1) * ROWS, :]
            own = (l == di) & (to_z == z)
            result = out_ref.at[0, x, :, cols]

            @pl.when(own)
            def _():
                pltpu.make_async_copy(tile, result, r_out).start()

            @pl.when(jnp.logical_not(own))
            def _():
                remote(tile, result, s_out.at[h, zz, l], r_out, (to_z * 4 + y, l))

            return 0

        lax.fori_loop(0, 8, finish, 0)

    forward(0)
    spread_head(1)
    relay(0)
    complete(0)
    prepare(0)
    work(0, 0, forward)
    relay(1)
    work(0, 1, complete)
    prepare(1)
    work(1, 0, None)
    work(1, 1, None)

    drain(out_ref, r_out)
    for h in range(2):
        for dx in range(4):
            if dx:
                drain(whole, s_kv.at[h, dx])
                drain(qbuf.at[0, pl.ds(0, 2)], s_q.at[h, dx])
            else:

                @pl.when(mine)
                def _():
                    drain(kva.at[0, 0, pl.ds(0, 3)], s_kv.at[h, dx])
                    drain(qbuf.at[0, pl.ds(0, 3), 0], s_q.at[h, dx])

                @pl.when(jnp.logical_not(mine))
                def _():
                    drain(whole, s_kv.at[h, dx])
                    drain(qbuf.at[0, pl.ds(0, 2)], s_q.at[h, dx])

    def sent(i, _):
        for h in range(2):
            for o in range(3):
                drain(whole, s_f.at[h, o, i])
            for o in range(5):
                drain(whole if o > 1 else part_of_one, s_r.at[h, o, i])
        return 0

    lax.fori_loop(0, 4, sent, 0)

    def returned(l, _):
        for h in range(2):
            for zz in range(2):

                @pl.when(jnp.logical_not((l == di) & (c + 2 * zz == z)))
                def _():
                    drain(obuf.at[0, 0, 0], s_out.at[h, zz, l])

        return 0

    lax.fori_loop(0, 8, returned, 0)


def per_device(query_rows, key_rows, value_rows, segment_ids):
    dma = pltpu.SemaphoreType.DMA
    vmem = pltpu.VMEM
    any_space = pl.BlockSpec(memory_space=pl.ANY)
    return pl.pallas_call(
        kernel,
        out_shape=jax.ShapeDtypeStruct((1, 4, ROWS, 4096), BF16),
        in_specs=[pl.BlockSpec(memory_space=vmem)] + [any_space] * 3,
        out_specs=any_space,
        scratch_shapes=[
            vmem((2, 8, 2, ROWS, SHARE * D), BF16),
            vmem((16, 2, 4, 2, ROWS, D), BF16),
            vmem((16, 2, 4, 2, ROWS, D), BF16),
            vmem((TILES, D, L), BF16),
            vmem((16, D, L), BF16),
            vmem((16, B, D), BF16),
            vmem((16, VR, B), BF16),
            vmem((2, B, D), BF16),
            vmem((2, B, L), jnp.float32),
            vmem((2, B, L), BF16),
            vmem((SLOTS, VR, L), jnp.float32),
            vmem((8, L), jnp.float32),
            vmem((2, 8, L), jnp.float32),
            vmem((2, 8, L), jnp.float32),
            vmem((2, 8, 2, ROWS, SHARE * D), BF16),
            pltpu.SMEM((8,), jnp.int32),
            dma((2, 4)), dma((2, 4)), dma((2, 4)), dma((2, 4)), dma((2, 3, 4)), dma((2, 2, 4)),
            dma((2, 5, 4)), dma((2, 2, 4)), dma((2, 4, 4)), dma((2, 2, 8)), dma(()),
        ],
        compiler_params=pltpu.CompilerParams(
            collective_id=0, has_side_effects=True, vmem_limit_bytes=60 * 2**20
        ),
    )(segment_ids, query_rows, key_rows, value_rows)


def solution(mesh):
    return jax.shard_map(
        per_device,
        mesh=mesh,
        in_specs=(
            P("dp", None, "grp", None),
            P("dp", None, "grp", None),
            P("dp", None, "grp", None),
            P(),
        ),
        out_specs=P("dp", None, "grp", None),
        check_vma=False,
    )
```

time: 124 us -> 107 us (0.86)
  the two profiles are of different devices: /device:TPU:89 before, /device:TPU:1 now
where the time goes in v3:
time: 107 us; the launch traced here: 106 us
  Pallas kernels  103 us (96%)
  local copies, waits for them, and re-layouts  3.13 us (3%)
    pallas_call x1, Pallas kernels, per_device(): pl.pallas_call(kernel, out_shape=jax.ShapeDtypeStruct((1, 4, ROWS, 4096),...  103 us
    unnamed x1, local copies, waits for them, and re-layouts  3.13 us

profile of v3, /device:TPU:1, one launch (start us, length us, event | category | flops | bytes accessed | tf_op | source)
XLA Modules:
  0.0 105.7 jit_solution(9218111558203042954)
XLA Ops:
  0.0 102.6 %shard_map.46 = bf16[1,4,64,4096]{3,2,1,0:T(8,128)(2,1)} custom-call(s32[4,8192]{1,0:T(4,128)} %seg_ref.1, bf16[1,4,64,4096]{3,2,1,0:T(8,128)(2,1)} %q_ref.1, bf16[1,4,64,1024]{3,2,1,0:T(8,128)(2,1)} %k_ref.1, bf16[1,4,64,1024]{3,2,1,0:T(8,128)(2,1)} %v_ref.1), custom_call_target="tpu_custom_call" | custom-call | tf_op jit(solution)/shard_map/pallas_call | solution.py:348
  102.6 3.1 %copy.6 = bf16[1,4,64,4096]{3,2,1,0:T(8,128)(2,1)} copy(bf16[1,4,64,4096]{3,2,1,0:T(8,128)(2,1)} %shard_map.46) | data formatting | bytes 4194304

commit v4 on v3

--- a/solution.py
+++ b/solution.py
@@ -176,7 +176,7 @@
     acc[0] = jnp.zeros((VR, L), jnp.float32)
     mref[...] = jnp.full_like(mref, -BIG)
 
-    def prepare(h):
+    def prepare_queries(h):
         def turn_queries(xs, _):
             drain(qbuf.at[0, pl.ds(0, 2)], r_q.at[h, xs])
             for t in range(4):
@@ -187,6 +187,7 @@
 
         lax.fori_loop(0, 4, turn_queries, 0)
 
+    def prepare(h):
         def turn_values(xs, _):
             for o in range(4):
                 drain(whole, r_s.at[h, o, xs])
@@ -212,7 +213,7 @@
             mask = ct[jnp.where(kb == 2 * l + zz, 0, 1)]
             left = jnp.concatenate([kv[kb, :, :, 0].reshape(B, D), kd[kb] + mask], axis=1)
             right = jnp.concatenate([qs[h * 16 + 2 * l + zz], qd[2 * l + zz]], axis=0)
-            s = jnp.dot(left, right, preferred_element_type=jnp.float32)
+            s = jnp.dot(left, right, preferred_element_type=jnp.float32) * FACTOR
             sbuf[par] = s
             mc[par, 0:1, :] = jnp.max(s, axis=0, keepdims=True)
 
@@ -220,8 +221,8 @@
             before = jnp.where(first == 1, -1e30, mref[0:1, :])
             top = jnp.maximum(before, mc[par, 0:1, :])
             mref[0:1, :] = top
-            alr[par, 0:1, :] = jnp.exp2((before - top) * FACTOR)
-            pbuf[par] = jnp.exp2(sbuf[par] * FACTOR - top * FACTOR).astype(BF16)
+            alr[par, 0:1, :] = jnp.exp2(before - top)
+            pbuf[par] = jnp.exp2(sbuf[par] - top).astype(BF16)
 
         def collect(i, kb, par):
             pv = jnp.dot(vt[kb], pbuf[par], preferred_element_type=jnp.float32)
@@ -291,11 +292,14 @@
     forward(0)
     spread_head(1)
     relay(0)
+    prepare_queries(0)
     complete(0)
+    forward(1)
     prepare(0)
-    work(0, 0, forward)
+    work(0, 0, None)
     relay(1)
     work(0, 1, complete)
+    prepare_queries(1)
     prepare(1)
     work(1, 0, None)
     work(1, 1, None)

time: 107 us -> 102 us (0.953); the launches traced: 106 us -> 102 us
  Pallas kernels: 103 us -> 98.8 us
    pallas_call x1, Pallas kernels: 103 us -> 98.8 us  [per_device(): pl.pallas_call(kernel, out_shape=jax.ShapeDtypeStruct((1, 4, ROWS, 4096),...]
where the time goes in v4:
time: 102 us
  Pallas kernels  98.8 us (97%)
  local copies, waits for them, and re-layouts  3.13 us (3%)
    pallas_call x1, Pallas kernels, per_device(): pl.pallas_call(kernel, out_shape=jax.ShapeDtypeStruct((1, 4, ROWS, 4096),...  98.8 us
    unnamed x1, local copies, waits for them, and re-layouts  3.13 us

profile of v4, /device:TPU:1, one launch (start us, length us, event | category | flops | bytes accessed | tf_op | source)
XLA Modules:
  0.0 102.0 jit_solution(7956334219701996054)
XLA Ops:
  0.0 98.8 %shard_map.46 = bf16[1,4,64,4096]{3,2,1,0:T(8,128)(2,1)} custom-call(s32[4,8192]{1,0:T(4,128)} %seg_ref.1, bf16[1,4,64,4096]{3,2,1,0:T(8,128)(2,1)} %q_ref.1, bf16[1,4,64,1024]{3,2,1,0:T(8,128)(2,1)} %k_ref.1, bf16[1,4,64,1024]{3,2,1,0:T(8,128)(2,1)} %v_ref.1), custom_call_target="tpu_custom_call" | custom-call | tf_op jit(solution)/shard_map/pallas_call | solution.py:352
  98.8 3.1 %copy.6 = bf16[1,4,64,4096]{3,2,1,0:T(8,128)(2,1)} copy(bf16[1,4,64,4096]{3,2,1,0:T(8,128)(2,1)} %shard_map.46) | data formatting | bytes 4194304

commit v5 on v4

--- a/solution.py
+++ b/solution.py
@@ -304,7 +304,6 @@
     work(1, 0, None)
     work(1, 1, None)
 
-    drain(out_ref, r_out)
     for h in range(2):
         for dx in range(4):
             if dx:
@@ -343,6 +342,7 @@
         return 0
 
     lax.fori_loop(0, 8, returned, 0)
+    drain(out_ref, r_out)
 
 
 def per_device(query_rows, key_rows, value_rows, segment_ids):

time: 102 us -> 102 us (level)
  no operation moved by 1% of the time
where the time goes in v5:
time: 102 us
  Pallas kernels  98.8 us (97%)
  local copies, waits for them, and re-layouts  3.13 us (3%)
    pallas_call x1, Pallas kernels, per_device(): pl.pallas_call(kernel, out_shape=jax.ShapeDtypeStruct((1, 4, ROWS, 4096),...  98.8 us
    unnamed x1, local copies, waits for them, and re-layouts  3.13 us

profile of v5, /device:TPU:1, one launch (start us, length us, event | category | flops | bytes accessed | tf_op | source)
XLA Modules:
  0.0 102.0 jit_solution(8486350516691075315)
XLA Ops:
  0.0 98.8 %shard_map.46 = bf16[1,4,64,4096]{3,2,1,0:T(8,128)(2,1)} custom-call(s32[4,8192]{1,0:T(4,128)} %seg_ref.1, bf16[1,4,64,4096]{3,2,1,0:T(8,128)(2,1)} %q_ref.1, bf16[1,4,64,1024]{3,2,1,0:T(8,128)(2,1)} %k_ref.1, bf16[1,4,64,1024]{3,2,1,0:T(8,128)(2,1)} %v_ref.1), custom_call_target="tpu_custom_call" | custom-call | tf_op jit(solution)/shard_map/pallas_call | solution.py:352
  98.8 3.1 %copy.6 = bf16[1,4,64,4096]{3,2,1,0:T(8,128)(2,1)} copy(bf16[1,4,64,4096]{3,2,1,0:T(8,128)(2,1)} %shard_map.46) | data formatting | bytes 4194304
